TPU v7x, 128 devices: a whole 4x4x4 slice. The times are simulated.
128 devices in a mesh: seg: 8 (over x_hi, z), seq: 16 (over x_lo, y, core).
Axes of the slice: x: 4 (x_hi: 2, x_lo: 2; x = x_hi * 2 + x_lo), y: 4, z: 4, core: 2. Of those that a mesh axis runs over, the one named last changes fastest.
Arguments:
- keyframe_latents: bfloat16 [8, 2048, 1536], P('seg', 'seq'), may hold values from -24 to 24
- keyframe_steps: int32 [8], P('seg'), may hold values from 0 to 63
- infill_latents: bfloat16 [8, 2, 2048, 1536], P('seg', None, 'seq'), may hold values from -24 to 24
- infill_steps: int32 [8, 2], P('seg'), may hold values from 0 to 63
- bounds: int32 [8, 2], P('seg'), may hold values from 0 to 7, as said below
- shift_table: float32 [64, 1536], replicated, may hold values from -4 to 4
- scale_table: float32 [64, 1536], replicated, may hold values from -0.5 to 1.5
- gate_table: float32 [64, 1536], replicated, may hold values from 0.5 to 2.5
- query_weight: bfloat16 [1536, 2048], P(None, 'seq'), may hold values from -0.15625 to 0.15625
- key_weight: bfloat16 [1536, 2048], P(None, 'seq'), may hold values from -0.15625 to 0.15625
- value_weight: bfloat16 [1536, 2048], P(None, 'seq'), may hold values from -0.15625 to 0.15625
- out_weight: bfloat16 [2048, 1536], P('seq'), may hold values from -0.125 to 0.125
- query_gain: float32 [128], replicated, may hold values from 0.5 to 2
- key_gain: float32 [128], replicated, may hold values from 0.5 to 2
Outputs:
- keyframe_out: bfloat16 [8, 2048, 1536], P('seg', 'seq')
- infill_out: bfloat16 [8, 2, 2048, 1536], P('seg', None, 'seq')
Inputs may be any that keep to these rules, and one draw needn't show every extreme that they name: `bounds`: the two keyframes of a segment differ.
All inputs are finite; a program needn't handle non-finite values.
Results may differ from a plain program's by a relative error of at most 0.0052.
Values may be sent and summed in bfloat16 or wider, within the bound.
A program may use at most 192 MiB of HBM per device.

v0:
```python
import math

import jax
import jax.numpy as jnp
from jax import lax
from jax.sharding import PartitionSpec as P

HEAD = 128


EPSILON = 1e-06


def lookup(steps, table):
    entries = table.shape[0]
    onehot = (steps[:, None] == jnp.arange(entries, dtype=jnp.int32)[None, :]).astype(jnp.float32)
    return jnp.dot(onehot, table, precision=lax.Precision.HIGHEST)


def modulate(latents, steps, shift_table, scale_table):
    shifts = lookup(steps, shift_table)
    scales = lookup(steps, scale_table)
    values = latents.astype(jnp.float32)
    center = values - jnp.mean(values, axis=-1, keepdims=True)
    normed = center * lax.rsqrt(jnp.mean(center * center, axis=-1, keepdims=True) + EPSILON)
    return (normed * (1.0 + scales[:, None, :]) + shifts[:, None, :]).astype(jnp.bfloat16)


def head_norm(projected, gain):
    flat_rows = projected.shape[0]
    shaped = projected.reshape(flat_rows, -1, gain.shape[0])
    normed = shaped * lax.rsqrt(jnp.mean(shaped * shaped, axis=-1, keepdims=True) + EPSILON) * gain
    return normed.reshape(flat_rows, -1).astype(jnp.bfloat16)


def project(modded, query_weight, key_weight, value_weight, query_gain, key_gain):
    frames, tokens, features = modded.shape
    flat = modded.reshape(frames * tokens, features)
    query_rows = head_norm(
        jnp.dot(flat, query_weight, preferred_element_type=jnp.float32), query_gain
    )
    key_rows = head_norm(jnp.dot(flat, key_weight, preferred_element_type=jnp.float32), key_gain)
    value_rows = jnp.dot(flat, value_weight, preferred_element_type=jnp.float32).astype(
        jnp.bfloat16
    )
    stacked = jnp.stack([query_rows, key_rows, value_rows], axis=1)
    return stacked.reshape(frames, tokens, 3, -1)


def attend(query_rows, key_rows, value_rows):
    length, columns = query_rows.shape
    head_count = columns // HEAD
    block_rows = math.gcd(512, length)
    query_blocks = query_rows.reshape(length // block_rows, block_rows, head_count, HEAD)
    key_heads = key_rows.reshape(-1, head_count, HEAD)
    value_heads = value_rows.reshape(-1, head_count, HEAD)

    def one_block(queries):
        scores = jnp.einsum(
            "qhd,khd->hqk", queries, key_heads, preferred_element_type=jnp.float32
        ) * (1.0 / math.sqrt(HEAD))
        powers = jnp.exp(scores)
        weights = (powers / jnp.sum(powers, axis=-1, keepdims=True)).astype(jnp.bfloat16)
        return jnp.einsum(
            "hqk,khd->qhd", weights, value_heads, preferred_element_type=jnp.float32
        ).astype(jnp.bfloat16)

    return lax.map(one_block, query_blocks).reshape(length, columns)


def local(
    keyframe_latents,
    keyframe_steps,
    infill_latents,
    infill_steps,
    bounds,
    shift_table,
    scale_table,
    gate_table,
    query_weight,
    key_weight,
    value_weight,
    out_weight,
    query_gain,
    key_gain,
):
    out_full = lax.all_gather(out_weight, "seq", axis=0, tiled=True)

    def to_heads(modded):
        return project(
            lax.all_gather(modded, "seq", axis=1, tiled=True),
            query_weight,
            key_weight,
            value_weight,
            query_gain,
            key_gain,
        )

    def finish(latents, steps, heads_out):
        token_side = lax.all_to_all(heads_out, "seq", split_axis=1, concat_axis=2, tiled=True)
        frames, tokens, columns = token_side.shape
        branch = jnp.dot(
            token_side.reshape(frames * tokens, columns),
            out_full,
            preferred_element_type=jnp.float32,
        ).reshape(latents.shape)
        gates = lookup(steps, gate_table)
        return (latents.astype(jnp.float32) + gates[:, None, :] * branch).astype(jnp.bfloat16)

    key_heads = to_heads(modulate(keyframe_latents, keyframe_steps, shift_table, scale_table))
    key_att = lax.map(
        lambda frame_data: attend(frame_data[:, 0], frame_data[:, 1], frame_data[:, 2]), key_heads
    )
    keyframe_out = finish(keyframe_latents, keyframe_steps, key_att)
    cond_all = lax.all_gather(key_heads[:, :, 1:], "seg", axis=0, tiled=True)
    segment_count = bounds.shape[0]
    length = cond_all.shape[1]
    picked = jnp.take(cond_all, bounds.reshape(-1), axis=0)
    picked = picked.reshape(segment_count, 2 * length, 2, cond_all.shape[3])
    frames = infill_latents.shape[1]
    flat_latents = infill_latents.reshape(
        segment_count * frames, infill_latents.shape[2], infill_latents.shape[3]
    )
    flat_steps = infill_steps.reshape(-1)
    infill_heads = to_heads(modulate(flat_latents, flat_steps, shift_table, scale_table))
    bounding = jnp.repeat(picked, frames, axis=0)

    def infill_frame(bundle):
        own_frame, cond_frame = bundle
        key_rows = jnp.concatenate([own_frame[:, 1], cond_frame[:, 0]], axis=0)
        value_rows = jnp.concatenate([own_frame[:, 2], cond_frame[:, 1]], axis=0)
        return attend(own_frame[:, 0], key_rows, value_rows)

    infill_att = lax.map(infill_frame, (infill_heads, bounding))
    infill_out = finish(flat_latents, flat_steps, infill_att).reshape(infill_latents.shape)
    return (keyframe_out, infill_out)


def solution(mesh):
    return jax.shard_map(
        local,
        mesh=mesh,
        in_specs=(
            P("seg", "seq", None),
            P("seg"),
            P("seg", None, "seq", None),
            P("seg", None),
            P("seg", None),
            P(),
            P(),
            P(),
            P(None, "seq"),
            P(None, "seq"),
            P(None, "seq"),
            P("seq", None),
            P(),
            P(),
        ),
        out_specs=(P("seg", "seq", None), P("seg", None, "seq", None)),
        check_vma=False,
    )
```

profile of v0, /device:TPU:1, one launch (start us, length us, event | category | flops | bytes accessed | tf_op | source)
XLA Modules:
  0.0 351.1 jit_solution(5878969197463367039)
XLA Ops:
  17.6 43.5 %all-gather.5.cloned.1.call-done = bf16[1,2048,1536]{2,1,0:T(8,128)(2,1)} async-done(((bf16[1,128,1536]{2,1,0:T(8,128)(2,1)}), bf16[1,2048,1536]{2,1,0:T(8,128)(2,1)}) %all-gather.5.cloned.1.call-update) | async-done | bytes 6291472 | tf_op jit(solution)/shard_map/all_gather | solution.py:91
  61.1 5.0 %multiply_reduce_fusion.2 = (f32[2048]{0:T(1024)S(1)}, f32[2048,128]{0,1:T(8,128)S(1)}) fusion(bf16[1536,128]{1,0:T(8,128)(2,1)S(1)} %copy-done.11, bf16[1,2048,1536]{2,1,0:T(8,128)(2,1)} %all-gather.5.cloned.1.call-done), kind=kOutput, calls=%fused_computation.81 | convolution fusion | flops 805828608 | bytes 7741440 | tf_op jit(solution)/shard_map/dot_general | solution.py:42
  66.5 4.8 %multiply_reduce_fusion.3 = (f32[2048]{0:T(1024)S(1)}, f32[2048,128]{1,0:T(8,128)S(1)}) fusion(bf16[1536,128]{1,0:T(8,128)(2,1)S(1)} %copy-done, bf16[1,2048,1536]{2,1,0:T(8,128)(2,1)} %all-gather.5.cloned.1.call-done), kind=kOutput, calls=%fused_computation.83 | convolution fusion | flops 805828608 | bytes 7741440 | tf_op jit(solution)/shard_map/dot_general | solution.py:40
  76.9 7.0 %while.37 = (s32[]{:T(128)}, bf16[4,512,1,128]{3,1,2,0:T(8,128)(2,1)S(1)}, bf16[4,512,1,128]{3,1,2,0:T(8,128)(2,1)S(1)}, bf16[2048,1,128]{2,0,1:T(8,128)(2,1)S(1)}, bf16[2048,1,128]{2,0,1:T(8,128)(2,1)S(1)}, /*index=5*/s32[]{:T(128)}) while((s32[]{:T(128)}, bf16[4,512,1,128]{3,1,2,0:T(8,128)(2,1)S(1)}, bf16[4,512,1,128]{3,1,2,0:T(8,128)(2,1)S(1)}, ...), condition=%wide.region_6.0_spmd, body=%wide.region_4.6_spmd.sunk | while | flops 542178816 | bytes 9703501 | solution.py:68
  84.0 8.1 %copy.65 = bf16[1,2048,128]{2,0,1:T(2,128)(2,1)S(1)} copy(bf16[1,2048,128]{2,1,0:T(8,128)(2,1)S(1)} %bitcast.242) | data formatting | bytes 1048576 | tf_op jit(solution)/shard_map/while/body/jit(dynamic_update_index_in_dim)/broadcast_in_dim | solution.py:111
  92.6 11.5 %reduce.21 = bf16[2048,128]{1,0:T(8,128)(2,1)S(1)} reduce(bf16[2048,1,128]{2,1,0:T(2,128)(2,1)S(1)} %bitcast.234, bf16[]{:T(256)} %broadcast.240), dimensions={1}, to_apply=%bitcast.196.reduce_sub_computation | reduce | bytes 1048578
  105.1 5.5 %all-to-all-start = ((bf16[16,2,8192]{2,1,0:T(2,128)(2,1)}), bf16[16,2,8192]{2,1,0:T(2,128)(2,1)}, u32[]{:S(2)}, u32[]{:S(2)}) async-start(bf16[16,2,8192]{2,1,0:T(2,128)(2,1)} %reshape.341), calls=%async_computation | async-start | bytes 1048576 | tf_op jit(solution)/shard_map/all_to_all | solution.py:100
  110.6 31.2 %all-gather.9.cloned.1.call-done = bf16[2,2048,1536]{2,1,0:T(8,128)(2,1)} async-done(((bf16[2,128,1536]{2,1,0:T(8,128)(2,1)}), bf16[2,2048,1536]{2,1,0:T(8,128)(2,1)}) %all-gather.9.cloned.1.call-update) | async-done | bytes 12582928 | tf_op jit(solution)/shard_map/all_gather | solution.py:91
  141.8 6.7 %multiply_reduce_fusion.1 = (f32[4096]{0:T(1024)S(1)}, f32[4096,128]{1,0:T(8,128)S(1)}) fusion(bf16[4096,1536]{1,0:T(8,128)(2,1)} %bitcast.246, bf16[1536,128]{1,0:T(8,128)(2,1)S(1)} %copy-done), kind=kOutput, calls=%fused_computation.63 | convolution fusion | flops 1611657216 | bytes 15089664 | tf_op jit(solution)/shard_map/dot_general | solution.py:40
  150.1 3.5 %multiply_reduce_fusion = (f32[4096]{0:T(1024)S(1)}, f32[4096,128]{1,0:T(8,128)S(1)}) fusion(bf16[4096,1536]{1,0:T(8,128)(2,1)S(1)} %bitcast.247, bf16[1536,128]{1,0:T(8,128)(2,1)S(1)} %copy-done.12), kind=kOutput, calls=%fused_computation.61 | convolution fusion | flops 1611657216 | bytes 15089664 | tf_op jit(solution)/shard_map/dot_general | solution.py:42
  153.7 3.4 convolution_convert_fusion
  160.6 91.0 %all-gather.11.cloned.1.call-done = bf16[8,2048,2,128]{3,1,2,0:T(8,128)(2,1)} async-done(((bf16[1,2048,2,128]{3,1,2,0:T(8,128)(2,1)}), bf16[8,2048,2,128]{3,1,2,0:T(8,128)(2,1)}) %all-gather.11.cloned.1.call-update) | async-done | bytes 8388624 | tf_op jit(solution)/shard_map/all_gather | solution.py:115
  251.6 4.3 %gather_fusion = bf16[2,2048,2,128]{3,1,2,0:T(8,128)(2,1)S(1)} fusion(bf16[8,2048,2,128]{3,1,2,0:T(8,128)(2,1)} %all-gather.11.cloned.1.call-done, s32[1024]{0:T(1024)S(1)} %pad_clamp_fusion), kind=kCustom, calls=%fused_computation | custom fusion | bytes 4194312 | tf_op jit(solution)/shard_map/jit(_take)/gather | solution.py:118
  256.1 2.2 bitcast_select_fusion
  258.2 2.5 reshape.321
  260.7 51.8 %while.39 = (s32[]{:T(128)}, bf16[2,2048,128]{2,1,0:T(8,128)(2,1)}, bf16[2,2048,3,128]{3,1,2,0:T(8,128)(2,1)}, bf16[2,4096,2,128]{3,1,2,0:T(8,128)(2,1)}, s32[]{:T(128)}, /*index=5*/s32[]{:T(128)}, s32[]{:T(128)}) while((s32[]{:T(128)}, bf16[2,2048,128]{2,1,0:T(8,128)(2,1)}, bf16[2,2048,3,128]{3,1,2,0:T(8,128)(2,1)}, ...), condition=%wide.region_15.16_spmd, body=%wide.region_11.15_spmd.sunk | while | flops 1632697856 | bytes 73667344 | solution.py:134
  265.4 20.4 %while.40 = (s32[]{:T(128)}, bf16[4,512,1,128]{3,1,2,0:T(8,128)(2,1)S(1)}, bf16[4,512,1,128]{3,1,2,0:T(8,128)(2,1)S(1)}, bf16[6144,1,128]{2,0,1:T(8,128)(2,1)S(1)}, bf16[6144,1,128]{2,0,1:T(8,128)(2,1)}, /*index=5*/s32[]{:T(128)}) while((s32[]{:T(128)}, bf16[4,512,1,128]{3,1,2,0:T(8,128)(2,1)S(1)}, bf16[4,512,1,128]{3,1,2,0:T(8,128)(2,1)S(1)}, ...), condition=%wide.region_14.14_spmd, body=%wide.region_12.13_spmd.sunk | while | flops 1626406400 | bytes 34869352 | solution.py:68
  267.4 3.1 fusion.115
  272.5 3.1 fusion.115
  277.6 3.1 fusion.115
  282.8 3.1 fusion.115
  291.2 20.4 %while.40 = (s32[]{:T(128)}, bf16[4,512,1,128]{3,1,2,0:T(8,128)(2,1)S(1)}, bf16[4,512,1,128]{3,1,2,0:T(8,128)(2,1)S(1)}, bf16[6144,1,128]{2,0,1:T(8,128)(2,1)S(1)}, bf16[6144,1,128]{2,0,1:T(8,128)(2,1)}, /*index=5*/s32[]{:T(128)}) while((s32[]{:T(128)}, bf16[4,512,1,128]{3,1,2,0:T(8,128)(2,1)S(1)}, bf16[4,512,1,128]{3,1,2,0:T(8,128)(2,1)S(1)}, ...), condition=%wide.region_14.14_spmd, body=%wide.region_12.13_spmd.sunk | while | flops 1626406400 | bytes 34869352 | solution.py:68
  293.3 3.1 fusion.115
  298.4 3.1 fusion.115
  303.5 3.1 fusion.115
  308.6 3.1 fusion.115
  312.5 3.6 %copy.59 = bf16[2,2048,128]{2,0,1:T(2,128)(2,1)} copy(bf16[2,2048,128]{2,1,0:T(8,128)(2,1)} %get-tuple-element.88) | data formatting | bytes 2097152 | tf_op jit(solution)/shard_map/while | solution.py:134
  316.2 5.4 %all-to-all-start.1 = ((bf16[2,2048,128]{2,0,1:T(2,128)(2,1)}), bf16[2,2048,128]{2,0,1:T(2,128)(2,1)S(1)}, u32[]{:S(2)}, u32[]{:S(2)}) async-start(bf16[2,2048,128]{2,0,1:T(2,128)(2,1)} %copy.59), calls=%async_computation.1 | async-start | bytes 2097152 | tf_op jit(solution)/shard_map/all_to_all | solution.py:100
  322.1 2.3 reshape.342
  324.8 4.6 %fusion.52 = bf16[1,128,1536]{2,1,0:T(8,128)(2,1)} fusion(bf16[128,2048]{0,1:T(8,128)(2,1)S(1)} %bitcast.239, bf16[2048,1536]{1,0:T(8,128)(2,1)} %all-gather.7.cloned.1.call-done, bf16[1,128,1536]{2,1,0:T(8,128)(2,1)S(1)} %copy-done.7, f32[1536]{0:T(1024)S(1)} %convolution_reduce_fusion.2), kind=kOutput, calls=%fused_computation.55 | convolution fusion | flops 806092800 | bytes 7608320 | tf_op jit(solution)/shard_map/dot_general | solution.py:102
  329.3 8.1 %all-to-all-done.1 = bf16[2,2048,128]{2,0,1:T(2,128)(2,1)S(1)} async-done(((bf16[2,2048,128]{2,0,1:T(2,128)(2,1)}), bf16[2,2048,128]{2,0,1:T(2,128)(2,1)S(1)}, u32[]{:S(2)}, u32[]{:S(2)}) %all-to-all-start.1) | async-done | bytes 1048608 | tf_op jit(solution)/shard_map/all_to_all | solution.py:100
  338.6 5.5 %fusion.48 = bf16[1,2,128,1536]{3,2,1,0:T(8,128)(2,1)} fusion(bf16[2,128,2048]{2,1,0:T(8,128)(2,1)S(1)} %dot_general.69, bf16[2048,1536]{1,0:T(8,128)(2,1)} %all-gather.7.cloned.1.call-done, bf16[1,2,128,1536]{3,2,1,0:T(8,128)(2,1)S(1)} %copy-done.6, f32[2,1536]{1,0:T(2,128)S(1)} %fusion.77), kind=kOutput, calls=%fused_computation.53 | convolution fusion | flops 1612185600 | bytes 8925184 | tf_op jit(solution)/shard_map/dot_general | solution.py:102
  (147 shorter events, 57.9 us)
Async XLA Ops:
  7.2 59.3 %copy-start = (bf16[1536,128]{1,0:T(8,128)(2,1)S(1)}, bf16[1536,128]{1,0:T(8,128)(2,1)}, u32[]{:S(2)}) copy-start(bf16[1536,128]{1,0:T(8,128)(2,1)} %param.28) | copy-start | bytes 1179652
  7.2 8.0 %copy-start.5 = (bf16[1,2,128,1536]{3,2,1,0:T(8,128)(2,1)S(1)}, bf16[1,2,128,1536]{3,2,1,0:T(8,128)(2,1)}, u32[]{:S(2)}) copy-start(bf16[1,2,128,1536]{3,2,1,0:T(8,128)(2,1)} %param.22) | copy-start | bytes 2359300
  7.2 53.9 %all-gather.5.cloned.1.call-start = ((), (), s32[]{:S(2)}) async-start(), calls=%async_computation.2 | async-start | bytes 6684672 | tf_op jit(solution)/shard_map/all_gather | solution.py:91
  9.2 6.5 %copy-start.8 = (f32[64,1536]{1,0:T(8,128)S(1)}, f32[64,1536]{1,0:T(8,128)}, u32[]{:S(2)}) copy-start(f32[64,1536]{1,0:T(8,128)} %param.26) | copy-start | bytes 1179652
  9.2 6.5 %copy-start.13 = (s32[1,2]{1,0:T(1,128)S(1)}, s32[1,2]{1,0:T(1,128)}, u32[]{:S(2)}) copy-start(s32[1,2]{1,0:T(1,128)} %param.23) | copy-start | bytes 28
  9.3 6.7 %copy-start.9 = (f32[64,1536]{1,0:T(8,128)S(1)}, f32[64,1536]{1,0:T(8,128)}, u32[]{:S(2)}) copy-start(f32[64,1536]{1,0:T(8,128)} %param.25) | copy-start | bytes 1179652
  15.1 126.7 %all-gather.9.cloned.1.call-start = ((), (), s32[]{:S(2)}) async-start(), calls=%async_computation.4 | async-start | bytes 13369344 | tf_op jit(solution)/shard_map/all_gather | solution.py:91
  15.3 45.8 %copy-start.11 = (bf16[1536,128]{1,0:T(8,128)(2,1)S(1)}, bf16[1536,128]{1,0:T(8,128)(2,1)}, u32[]{:S(2)}) copy-start(bf16[1536,128]{1,0:T(8,128)(2,1)} %param.29) | copy-start | bytes 1179652
  17.5 234.1 %all-gather.11.cloned.1.call-start = ((), (), s32[]{:S(2)}) async-start(), calls=%async_computation.5 | async-start | bytes 9437184 | tf_op jit(solution)/shard_map/all_gather | solution.py:115
  66.4 4.9 %copy-start.4 = (bf16[1,2048,1536]{2,1,0:T(8,128)(2,1)S(1)}, bf16[1,2048,1536]{2,1,0:T(8,128)(2,1)}, u32[]{:S(2)}) copy-start(bf16[1,2048,1536]{2,1,0:T(8,128)(2,1)} %all-gather.5.cloned.1.call-done) | copy-start | bytes 18874372
  66.4 4.9 %copy-start.20 = (bf16[1536,128]{1,0:T(8,128)(2,1)S(1)}, bf16[1536,128]{1,0:T(8,128)(2,1)}, u32[]{:S(2)}) copy-start(bf16[1536,128]{1,0:T(8,128)(2,1)} %param.30) | copy-start | bytes 1179652
  71.3 2.2 copy-start.17
  75.2 249.6 %all-gather.7.cloned.1.call-start = ((), (), s32[]{:S(2)}) async-start(), calls=%async_computation.3 | async-start | bytes 6684672 | tf_op jit(solution)/shard_map/all_gather | solution.py:87
  105.1 211.1 %all-to-all-start = ((bf16[16,2,8192]{2,1,0:T(2,128)(2,1)}), bf16[16,2,8192]{2,1,0:T(2,128)(2,1)}, u32[]{:S(2)}, u32[]{:S(2)}) async-start(bf16[16,2,8192]{2,1,0:T(2,128)(2,1)} %reshape.341), calls=%async_computation | async-start | bytes 1048576 | tf_op jit(solution)/shard_map/all_to_all | solution.py:100
  141.8 6.7 %copy-start.12 = (bf16[1536,128]{1,0:T(8,128)(2,1)S(1)}, bf16[1536,128]{1,0:T(8,128)(2,1)}, u32[]{:S(2)}) copy-start(bf16[1536,128]{1,0:T(8,128)(2,1)} %param.29) | copy-start | bytes 1179652
  141.8 8.3 %copy-start.19 = (bf16[2,2048,1536]{2,1,0:T(8,128)(2,1)S(1)}, bf16[2,2048,1536]{2,1,0:T(8,128)(2,1)}, u32[]{:S(2)}) copy-start(bf16[2,2048,1536]{2,1,0:T(8,128)(2,1)} %all-gather.9.cloned.1.call-done) | copy-start | bytes 37748740
  150.1 3.5 %copy-start.21 = (bf16[1536,128]{1,0:T(8,128)(2,1)S(1)}, bf16[1536,128]{1,0:T(8,128)(2,1)}, u32[]{:S(2)}) copy-start(bf16[1536,128]{1,0:T(8,128)(2,1)} %param.30) | copy-start | bytes 1179652
  153.6 3.5 copy-start.16
  261.0 2.7 copy-start.2
  270.5 2.0 copy-start.3
  275.6 2.0 copy-start.3
  280.7 2.0 copy-start.3
  286.7 2.8 copy-start.2
  291.2 2.0 copy-start.3
  296.3 2.0 copy-start.3
  301.5 2.0 copy-start.3
  306.6 2.0 copy-start.3
  312.5 9.1 %copy-start.10 = (f32[64,1536]{1,0:T(8,128)S(1)}, f32[64,1536]{1,0:T(8,128)}, u32[]{:S(2)}) copy-start(f32[64,1536]{1,0:T(8,128)} %param.27) | copy-start | bytes 1179652
  312.5 9.3 %copy-start.14 = (s32[1,2]{1,0:T(1,128)S(1)}, s32[1,2]{1,0:T(1,128)}, u32[]{:S(2)}) copy-start(s32[1,2]{1,0:T(1,128)} %param.23) | copy-start | bytes 28
  316.2 21.2 %all-to-all-start.1 = ((bf16[2,2048,128]{2,0,1:T(2,128)(2,1)}), bf16[2,2048,128]{2,0,1:T(2,128)(2,1)S(1)}, u32[]{:S(2)}, u32[]{:S(2)}) async-start(bf16[2,2048,128]{2,0,1:T(2,128)(2,1)} %copy.59), calls=%async_computation.1 | async-start | bytes 2097152 | tf_op jit(solution)/shard_map/all_to_all | solution.py:100
  322.1 2.7 copy-start.7
  338.6 5.5 %copy-start.1 = (bf16[1536,128]{1,0:T(8,128)(2,1)S(1)}, bf16[1536,128]{1,0:T(8,128)(2,1)}, u32[]{:S(2)}) copy-start(bf16[1536,128]{1,0:T(8,128)(2,1)} %param.28) | copy-start | bytes 1179652
  (5 other events, 7.5 us)
Sparse Core Ops, SparseCore 0:
  15.2 45.8 all-gather.4
  63.3 78.4 all-gather.8
  144.2 107.3 all-gather.10
  253.1 40.8 all-gather.6
where the time goes:
time: 357 us; the launch traced here: 351 us
  waiting for transfers between devices  174 us (49%)
  matrix products  86.5 us (24%)
  local copies, waits for them, and re-layouts  34.9 us (10%)
  other arithmetic  28.3 us (8%)
  between operations  15.5 us (4%)
  starting transfers between devices  11.2 us (3%)
    all_gather x1, waiting for transfers between devices, local(): cond_all = lax.all_gather(key_heads[:, :, 1:], 'seg', axis=0, tiled=True)  91 us
    all_gather x2, waiting for transfers between devices, to_heads(): lax.all_gather(modded, 'seq', axis=1, tiled=True)  74.7 us
    dot_general x12, matrix products, one_block(): jnp.einsum('hqk,khd->qhd', weights, value_heads, preferred_element_type=j...  28 us
    dot_general x12, matrix products, one_block(): jnp.einsum('qhd,khd->hqk', queries, key_heads, preferred_element_type=jnp...  19.6 us
    unnamed x1, other arithmetic  11.5 us
    dot_general x2, matrix products, project(): jnp.dot(flat, query_weight, preferred_element_type=jnp.float32)  11.5 us
    all_to_all x2, starting transfers between devices, finish(): lax.all_to_all(heads_out, 'seq', split_axis=1, concat_axis=2, tiled=True)  10.9 us
    dot_general x2, matrix products, finish(): jnp.dot(token_side.reshape(frames * tokens, columns), out_full, preferred...  10.1 us
  transfers between devices with their start and end apart: 6, of which 4 were waited for; matrix products, arithmetic and copies ran while one was open for 38% of the time, Pallas kernels for 0%

commit v1 on v0

v1 whole, which is shorter than its diff:
```python
import math

import jax
import jax.numpy as jnp
from jax import lax
from jax.experimental import pallas as pl
from jax.experimental.pallas import tpu as pltpu
from jax.sharding import PartitionSpec as P

MESH = pl.DeviceIdType.MESH
HEAD = 128
TOK = 128
SLOTS = 16
D = 1536
EPSILON = 1e-06
QSCALE = math.log2(math.e) / math.sqrt(HEAD)
OFFSETS = [(0, 0), (0, 3), (0, 1), (1, 0), (0, 2), (1, 3), (1, 1), (1, 2)]
POS = {o: i for i, o in enumerate(OFFSETS)}
CHUNKS = [(0, 2), (2, 8), (8, 12), (12, 16)]
PARTS = [(0, 8), (8, 12), (12, 16)]
QB = 512
KB = 512


def kernel(
    key_lat, inf_lat, key_steps, inf_steps, bounds, shift, scale, gate, wq, wk, wv, wo, qgain, kgain,
    key_out, inf_out,
    G, KV0, KV1, KV2, KO, Q, ACC, ATT, AR, W,
    g_send, g_recv, k_send, k_recv, a_send, a_recv,
):
    seg, seq = lax.axis_index("seg"), lax.axis_index("seq")
    xh, z = seg // 4, seg % 4
    xl, y, core = seq // 8, (seq // 2) % 4, seq % 2

    def at_seq(dx, dy, dc):
        x2 = 1 - xl if dx else xl
        c2 = 1 - core if dc else core
        return (seg, x2 * 8 + ((y + dy) % 4) * 2 + c2)

    def at_seg(dx, dz):
        x2 = 1 - xh if dx else xh
        return (x2 * 4 + (z + dz) % 4, seq)

    peers = [at_seq(*OFFSETS[r // 2], r % 2) for r in range(1, SLOTS)]
    peers += [at_seg(0, 1), at_seg(0, 3), at_seg(1, 0)]
    barrier = pltpu.get_barrier_semaphore()
    for peer in peers:
        pl.semaphore_signal(barrier, inc=1, device_id=peer, device_id_type=MESH)

    def g_copy(f, src, to, dst, sem, rows=None):
        a, b = G.at[f, src], G.at[f, dst]
        if rows is not None:
            a, b = G.at[f, src, pl.ds(*rows)], G.at[f, dst, pl.ds(*rows)]
        return pltpu.make_async_remote_copy(
            src_ref=a, dst_ref=b, send_sem=g_send.at[f], recv_sem=g_recv.at[f, sem],
            device_id=at_seq(*to), device_id_type=MESH,
        )

    LOW, HIGH = (0, TOK // 2), (TOK // 2, TOK // 2)
    S = {o: 2 * i for o, i in POS.items()}

    def send(f, src, to, dst, sem=None, rows=None):
        g_copy(f, src, to, dst, dst if sem is None else sem, rows).start()

    def took(f, slot, sem=None, rows=None):
        g_copy(f, slot, (0, 1, 0), slot, slot if sem is None else sem, rows).wait_recv()

    def sib(f, o):
        send(f, S[o], (0, 0, 1), S[o] + 1)

    def g_send_sib(f):
        sib(f, (0, 0))

    def g_send_y(f):
        send(f, 0, (0, 1, 0), S[0, 3])
        send(f, 0, (0, 3, 0), S[0, 1])

    def g_send_x(f):
        send(f, 0, (1, 0, 0), S[1, 0])

    def g_fwd_y(f):
        took(f, S[0, 3])
        send(f, S[0, 3], (0, 1, 0), S[0, 2], rows=LOW)
        sib(f, (0, 3))
        took(f, S[0, 1])
        send(f, S[0, 1], (0, 3, 0), S[0, 2], sem=16, rows=HIGH)
        sib(f, (0, 1))

    def g_fwd_x(f):
        took(f, S[1, 0])
        send(f, S[1, 0], (0, 1, 0), S[1, 3])
        send(f, S[1, 0], (0, 3, 0), S[1, 1])
        sib(f, (1, 0))

    def g_fwd_2(f):
        took(f, S[0, 2], rows=LOW)
        took(f, S[0, 2], sem=16, rows=HIGH)
        send(f, S[0, 2], (1, 0, 0), S[1, 2])
        sib(f, (0, 2))

    def g_fwd_3(f):
        took(f, S[1, 3])
        sib(f, (1, 3))
        took(f, S[1, 1])
        sib(f, (1, 1))

    def g_fwd_4(f):
        took(f, S[1, 2])
        sib(f, (1, 2))

    def g_sib(f, lo, hi):
        for r in range(lo, hi, 2):
            took(f, r + 1)

    KV = [KV0, KV1, KV2]

    def part_of(slot):
        n = [n for n, (lo, hi) in enumerate(PARTS) if lo <= slot < hi][0]
        return KV[n], PARTS[n][0]

    def k_copy(m, src, to, dst, sem, half=None):
        lo, hi = CHUNKS[m]
        part, base = part_of(lo)
        start, size = (lo - base) * TOK, (hi - lo) * TOK
        if half is not None:
            size //= 2
            start += half * size
        rows = pl.ds(start, size)
        return pltpu.make_async_remote_copy(
            src_ref=part.at[src, rows], dst_ref=part.at[dst, rows], send_sem=k_send.at[m], recv_sem=k_recv.at[m, sem],
            device_id=at_seg(*to), device_id_type=MESH,
        )

    def k_took(m, slot, sem=None, half=None):
        k_copy(m, slot, (0, 1), slot, slot if sem is None else sem, half).wait_recv()

    def k_send_0(m):
        k_copy(m, 0, (1, 0), POS[1, 0], POS[1, 0]).start()
        k_copy(m, 0, (0, 1), POS[0, 3], POS[0, 3]).start()
        k_copy(m, 0, (0, 3), POS[0, 1], POS[0, 1]).start()

    def k_fwd_1(m):
        k_took(m, POS[0, 3])
        k_copy(m, POS[0, 3], (0, 1), POS[0, 2], POS[0, 2], 0).start()
        k_took(m, POS[0, 1])
        k_copy(m, POS[0, 1], (0, 3), POS[0, 2], 8, 1).start()
        k_took(m, POS[1, 0])
        k_copy(m, POS[1, 0], (0, 1), POS[1, 3], POS[1, 3]).start()
        k_copy(m, POS[1, 0], (0, 3), POS[1, 1], POS[1, 1]).start()

    def k_fwd_2(m):
        k_took(m, POS[1, 3])
        k_copy(m, POS[1, 3], (0, 1), POS[1, 2], POS[1, 2], 0).start()
        k_took(m, POS[1, 1])
        k_copy(m, POS[1, 1], (0, 3), POS[1, 2], 9, 1).start()

    def k_done(m):
        k_took(m, POS[0, 2], half=0)
        k_took(m, POS[0, 2], sem=8, half=1)
        k_took(m, POS[1, 2], half=0)
        k_took(m, POS[1, 2], sem=9, half=1)

    def modulate(f):
        step = key_steps[0] if f == 0 else inf_steps[0, f - 1]
        gain = 1.0 + scale[pl.ds(step, 1), :]
        move = shift[pl.ds(step, 1), :]

        @pl.loop(0, TOK, step=32)
        def _(r):
            rows = pl.ds(r, 32)
            x = (key_lat[0, rows, :] if f == 0 else inf_lat[0, f - 1, rows, :]).astype(jnp.float32)
            x = x - jnp.mean(x, axis=-1, keepdims=True)
            x = x * lax.rsqrt(jnp.mean(x * x, axis=-1, keepdims=True) + EPSILON)
            G[f, 0, rows, :] = (x * gain + move).astype(jnp.bfloat16)

    qg = qgain[...].reshape(1, HEAD) * QSCALE
    kg = kgain[...].reshape(1, HEAD)

    def project(f, lo, hi):
        @pl.loop(lo // 2, hi // 2)
        def _(i):
            x = G[f, pl.ds(2 * i, 2)].reshape(2 * TOK, D)
            r = jnp.dot(x, W[...], preferred_element_type=jnp.float32)
            rows = pl.ds(pl.multiple_of(i * 2 * TOK, 2 * TOK), 2 * TOK)

            def norm(t, gain):
                return (t * lax.rsqrt(jnp.mean(t * t, axis=-1, keepdims=True) + EPSILON) * gain).astype(jnp.bfloat16)

            Q[f, rows, :] = norm(r[:, :HEAD], qg)
            kv = jnp.concatenate([norm(r[:, HEAD : 2 * HEAD], kg), r[:, 2 * HEAD :].astype(jnp.bfloat16)], axis=1)
            if f == 0:
                part, base = part_of(lo)
                part[0, pl.ds(pl.multiple_of((i - base // 2) * 2 * TOK, 2 * TOK), 2 * TOK), :] = kv
            else:
                KO[f - 1, rows, :] = kv

    ones = jnp.ones((KB, HEAD), jnp.bfloat16)

    def a_copy(f, r):
        o = OFFSETS[r // 2]
        back = 2 * POS[o[0], (4 - o[1]) % 4] + r % 2
        return pltpu.make_async_remote_copy(
            src_ref=ATT.at[f, r], dst_ref=AR.at[f, :, pl.ds(back * HEAD, HEAD)], send_sem=a_send.at[f],
            recv_sem=a_recv.at[f], device_id=at_seq(*o, r % 2), device_id_type=MESH,
        )

    def attend(f, lo, hi, sources, first, last, hooks=None):
        @pl.loop(lo, hi)
        def _(i):
            rows = pl.ds(pl.multiple_of(i * QB, QB), QB)
            q = Q[f, rows, :]
            a = None if first else ACC[f - 1, rows, :]
            for load in sources:
                kv = load()
                s = lax.dot_general(q, kv[:, :HEAD], (((1,), (1,)), ((), ())), preferred_element_type=jnp.float32)
                p = jnp.exp2(s).astype(jnp.bfloat16)
                v = jnp.concatenate([kv[:, HEAD:], ones], axis=1)
                t = jnp.dot(p, v, preferred_element_type=jnp.float32)
                a = t if a is None else a + t
            if not last:
                ACC[f - 1, rows, :] = a
            else:
                o = (a[:, :HEAD] / a[:, HEAD:]).astype(jnp.bfloat16)
                per = QB // TOK
                ATT[f, pl.ds(i * per, per)] = o.reshape(per, TOK, HEAD)
                for n in range(lo, hi):

                    @pl.when(i == n)
                    def _(n=n):
                        for r in range(n * per, (n + 1) * per):
                            if r == 0:
                                AR[f, :, 0:HEAD] = o[:TOK]
                            else:
                                a_copy(f, r).start()

            for n, hook in (hooks or {}).items():

                @pl.when(i == n)
                def _(hook=hook):
                    for h in hook:
                        h[0](*h[1:])

    def own(f):
        if f == 0:
            return [
                lambda n=n, j=j: KV[n][0, j * KB : (j + 1) * KB, :]
                for n, (lo, hi) in enumerate(PARTS)
                for j in range((hi - lo) * TOK // KB)
            ]
        return [lambda j=j: KO[f - 1, j * KB : (j + 1) * KB, :] for j in range(SLOTS * TOK // KB)]

    def slot_of(k):
        kx, kz = k // 4, k % 4
        dx = jnp.where(kx == xh, 0, 1)
        dz = (kz - z + 4) % 4
        slot = jnp.int32(0)
        for o, i in POS.items():
            slot = jnp.where((dx == o[0]) & (dz == o[1]), i, slot)
        return slot

    ends = [slot_of(bounds[0, 0]), slot_of(bounds[0, 1])]

    def cond(*parts):
        return [
            lambda n=n, t=t, j=j: KV[n][t, j * KB : (j + 1) * KB, :]
            for n in parts
            for j in range((PARTS[n][1] - PARTS[n][0]) * TOK // KB)
            for t in ends
        ]

    def finish():
        x = AR[...].reshape(3 * TOK, SLOTS * HEAD)

        @pl.loop(0, D // 256)
        def _(n):
            cols = pl.ds(pl.multiple_of(n * 256, 256), 256)
            w = G[3, :, :, cols].reshape(SLOTS * TOK, 256)
            t = jnp.dot(x, w, preferred_element_type=jnp.float32)
            for f in range(3):
                s = key_steps[0] if f == 0 else inf_steps[0, f - 1]
                g = gate[pl.ds(s, 1), cols]
                lat = (key_lat[0, :, cols] if f == 0 else inf_lat[0, f - 1, :, cols]).astype(jnp.float32)
                o = (lat + g * t[f * TOK : (f + 1) * TOK]).astype(jnp.bfloat16)
                if f == 0:
                    key_out[0, :, cols] = o
                else:
                    inf_out[0, f - 1, :, cols] = o

    modulate(0)
    pl.semaphore_wait(barrier, len(peers))
    g_send_sib(0)
    g_send_y(0)
    g_send_x(0)
    W[:, :HEAD] = wq[...]
    W[:, HEAD : 2 * HEAD] = wk[...]
    W[:, 2 * HEAD :] = wv[...]
    modulate(1)
    g_send_sib(1)
    g_sib(0, 0, 2)
    project(0, 0, 2)
    k_send_0(0)
    modulate(2)
    g_send_sib(2)
    G[3, 0] = wo[...]
    g_send_sib(3)

    g_fwd_y(0)
    g_fwd_x(0)
    g_send_x(1)
    k_fwd_1(0)
    g_sib(0, 2, 8)
    project(0, 2, 8)
    k_send_0(1)
    g_fwd_2(0)
    k_fwd_2(0)
    g_send_y(1)
    g_fwd_3(0)
    k_fwd_1(1)
    g_sib(0, 8, 12)
    project(0, 8, 12)
    k_send_0(2)
    g_fwd_4(0)
    g_sib(0, 12, 16)
    project(0, 12, 16)
    k_send_0(3)
    g_send_x(2)
    attend(0, 0, 4, own(0), True, True, {1: [(g_fwd_y, 1), (g_fwd_x, 1)], 2: [(k_fwd_2, 1)]})
    g_sib(1, 0, 8)
    project(1, 0, 8)
    g_fwd_2(1)
    g_send_y(2)
    k_fwd_1(2)
    k_done(0)
    k_done(1)
    attend(1, 0, 2, cond(0), True, False, {0: [(g_fwd_3, 1)]})
    g_fwd_4(1)
    g_send_x(3)
    k_fwd_2(2)
    g_sib(1, 8, 16)
    project(1, 8, 16)
    attend(1, 0, 2, own(1), False, False, {0: [(g_fwd_y, 2), (g_fwd_x, 2)]})
    k_fwd_1(3)
    attend(1, 2, 4, own(1), True, False, {2: [(g_fwd_2, 2)]})
    g_send_y(3)
    g_sib(2, 0, 8)
    project(2, 0, 8)
    k_done(2)
    attend(1, 2, 4, cond(0), False, False, {2: [(k_fwd_2, 3)]})
    attend(2, 0, 2, cond(0), True, False, {0: [(g_fwd_3, 2)]})
    g_fwd_4(2)
    g_sib(2, 8, 16)
    project(2, 8, 16)
    attend(2, 0, 2, own(2), False, False, {0: [(g_fwd_y, 3), (g_fwd_x, 3)]})
    attend(2, 2, 4, own(2), True, False, {2: [(g_fwd_2, 3)]})
    attend(2, 2, 4, cond(0), False, False)
    k_done(3)
    attend(1, 0, 4, cond(1, 2), False, True, {1: [(g_fwd_3, 3)], 3: [(g_fwd_4, 3)]})
    attend(2, 0, 4, cond(1, 2), False, True)
    g_sib(3, 0, 16)
    for f in range(3):
        whole = AR.at[f, :, pl.ds(HEAD, (SLOTS - 1) * HEAD)]
        pltpu.make_async_remote_copy(
            src_ref=whole, dst_ref=whole, send_sem=a_send.at[f], recv_sem=a_recv.at[f],
            device_id=at_seq(0, 1, 0), device_id_type=MESH,
        ).wait_recv()
    finish()

    for f in range(4):
        sent = G.at[f, pl.ds(0, 15)]
        pltpu.make_async_remote_copy(
            src_ref=sent, dst_ref=sent, send_sem=g_send.at[f], recv_sem=g_recv.at[f, 0],
            device_id=at_seq(0, 1, 0), device_id_type=MESH,
        ).wait_send()
    for m, (lo, hi) in enumerate(CHUNKS):
        part, base = part_of(lo)
        sent = part.at[pl.ds(0, 7), pl.ds((lo - base) * TOK, (hi - lo) * TOK)]
        pltpu.make_async_remote_copy(
            src_ref=sent, dst_ref=sent, send_sem=k_send.at[m], recv_sem=k_recv.at[m, 0],
            device_id=at_seg(0, 1), device_id_type=MESH,
        ).wait_send()
    for f in range(3):
        sent = ATT.at[f, pl.ds(1, 15)]
        pltpu.make_async_remote_copy(
            src_ref=sent, dst_ref=sent, send_sem=a_send.at[f], recv_sem=a_recv.at[f],
            device_id=at_seq(0, 1, 0), device_id_type=MESH,
        ).wait_send()


def local(
    keyframe_latents, keyframe_steps, infill_latents, infill_steps, bounds, shift_table, scale_table, gate_table,
    query_weight, key_weight, value_weight, out_weight, query_gain, key_gain,
):
    vmem, smem = pl.BlockSpec(memory_space=pltpu.VMEM), pl.BlockSpec(memory_space=pltpu.SMEM)
    bf16, f32 = jnp.bfloat16, jnp.float32
    n_tok = SLOTS * TOK
    return pl.pallas_call(
        kernel,
        name="diffusion_block",
        out_shape=(
            jax.ShapeDtypeStruct(keyframe_latents.shape, bf16),
            jax.ShapeDtypeStruct(infill_latents.shape, bf16),
        ),
        in_specs=[vmem, vmem, smem, smem, smem] + [vmem] * 9,
        out_specs=(vmem, vmem),
        scratch_shapes=[
            pltpu.VMEM((4, SLOTS, TOK, D), bf16),
            *[pltpu.VMEM((8, (hi - lo) * TOK, 2 * HEAD), bf16) for lo, hi in PARTS],
            pltpu.VMEM((2, n_tok, 2 * HEAD), bf16),
            pltpu.VMEM((3, n_tok, HEAD), bf16),
            pltpu.VMEM((2, n_tok, 2 * HEAD), f32),
            pltpu.VMEM((3, SLOTS, TOK, HEAD), bf16),
            pltpu.VMEM((3, TOK, SLOTS * HEAD), bf16),
            pltpu.VMEM((D, 3 * HEAD), bf16),
            pltpu.SemaphoreType.DMA((4,)),
            pltpu.SemaphoreType.DMA((4, 17)),
            pltpu.SemaphoreType.DMA((4,)),
            pltpu.SemaphoreType.DMA((4, 10)),
            pltpu.SemaphoreType.DMA((3,)),
            pltpu.SemaphoreType.DMA((3,)),
        ],
        compiler_params=pltpu.CompilerParams(
            collective_id=0, has_side_effects=True, vmem_limit_bytes=62 * 2**20
        ),
    )(
        keyframe_latents, infill_latents, keyframe_steps, infill_steps, bounds, shift_table, scale_table, gate_table,
        query_weight, key_weight, value_weight, out_weight, query_gain, key_gain,
    )


def solution(mesh):
    return jax.shard_map(
        local,
        mesh=mesh,
        in_specs=(
            P("seg", "seq", None), P("seg"), P("seg", None, "seq", None), P("seg", None), P("seg", None),
            P(), P(), P(), P(None, "seq"), P(None, "seq"), P(None, "seq"), P("seq", None), P(), P(),
        ),
        out_specs=(P("seg", "seq", None), P("seg", None, "seq", None)),
        check_vma=False,
    )
```

time: 357 us -> 150 us (0.42); the launches traced: 351 us -> 150 us
  waiting for transfers between devices: 174 us -> 0 us
  Pallas kernels: 0 us -> 146 us
  matrix products: 86.5 us -> 0 us
  local copies, waits for them, and re-layouts: 34.9 us -> 2.72 us
  other arithmetic: 28.3 us -> 0 us
  between operations: 15.5 us -> 1.3 us
  starting transfers between devices: 11.2 us -> 0 us
    all_gather x4 -> x0, waiting for transfers between devices: 166 us -> none  [the longest x1 91 us: local(): cond_all = lax.all_gather(key_heads[:, :, 1:], 'seg', axis=0, tiled=True)]
    pallas_call x0 -> x1, Pallas kernels: none -> 146 us  [local(): pl.pallas_call(kernel, name='diffusion_block', out_shape=(jax.ShapeDtypeS...]
    dot_general x38 -> x0, matrix products: 86.5 us -> none  [the longest x12 28 us: one_block(): jnp.einsum('hqk,khd->qhd', weights, value_heads, preferred_element_type=j...]
    unnamed x1 -> x0, other arithmetic: 11.5 us -> none
    all_to_all x2 -> x0, starting transfers between devices: 10.9 us -> none  [finish(): lax.all_to_all(heads_out, 'seq', split_axis=1, concat_axis=2, tiled=True)]
    broadcast_in_dim x3 -> x0, local copies, waits for them, and re-layouts: 8.24 us -> none  [the longest x1 8.14 us: local(): lax.map(lambda frame_data: attend(frame_data[:, 0], frame_data[:, 1], fra...]
    all_to_all x2 -> x0, waiting for transfers between devices: 8.06 us -> none  [finish(): lax.all_to_all(heads_out, 'seq', split_axis=1, concat_axis=2, tiled=True)]
    convert_element_type x7 -> x0, other arithmetic: 6.41 us -> none  [the longest x2 3.3 us: modulate(): (normed * (1.0 + scales[:, None, :]) + shifts[:, None, :]).astype(jnp.bfl...]
  transfers between devices with their start and end apart: 6 -> 0, of which waited for: 4 -> 0; matrix products, arithmetic and copies ran while one was open for 38% -> 0% of each run, Pallas kernels for 0% -> 0%
where the time goes in v1:
time: 150 us
  Pallas kernels  146 us (97%)
  local copies, waits for them, and re-layouts  2.72 us (2%)
    pallas_call x1, Pallas kernels, local(): pl.pallas_call(kernel, name='diffusion_block', out_shape=(jax.ShapeDtypeS...  146 us

profile of v1, /device:TPU:1, one launch (start us, length us, event | category | flops | bytes accessed | tf_op | source)
XLA Modules:
  0.0 149.9 jit_solution(4008877168195850597)
XLA Ops:
  1.3 145.9 %diffusion_block.1 = (bf16[1,128,1536]{2,1,0:T(8,128)(2,1)}, bf16[1,2,128,1536]{3,2,1,0:T(8,128)(2,1)}) custom-call(bf16[1,128,1536]{2,1,0:T(8,128)(2,1)} %key_lat.1, bf16[1,2,128,1536]{3,2,1,0:T(8,128)(2,1)} %inf_lat.1, s32[1]{0:T(128)S(6)} %copy.18.key_steps, s32[1,2]{1,0:T(1,128)} %inf_steps.1, s32[1,2]{1,0:T(1,128)} %bounds.1, f32[64,1536]{1,0:T(8,128)} %shift.1, ...), custom_call_target="tpu_custom_call" | custom-call | tf_op jit(solution)/shard_map/diffusion_block/pallas_call | solution.py:396
  147.2 0.0 copy-start
  147.2 1.8 %copy.19 = bf16[1,128,1536]{2,1,0:T(8,128)(2,1)} copy(bf16[1,128,1536]{2,1,0:T(8,128)(2,1)} %get-tuple-element.4) | data formatting | bytes 786432
  149.0 0.0 copy-done
  149.0 0.9 copy.20
Async XLA Ops:
  147.2 1.9 %copy-start = (bf16[1,2,128,1536]{3,2,1,0:T(8,128)(2,1)S(1)}, bf16[1,2,128,1536]{3,2,1,0:T(8,128)(2,1)}, u32[]{:S(2)}) copy-start(bf16[1,2,128,1536]{3,2,1,0:T(8,128)(2,1)} %get-tuple-element.5) | copy-start | bytes 2359300

commit v2 on v1

--- a/solution.py
+++ b/solution.py
@@ -16,17 +16,44 @@
 QSCALE = math.log2(math.e) / math.sqrt(HEAD)
 OFFSETS = [(0, 0), (0, 3), (0, 1), (1, 0), (0, 2), (1, 3), (1, 1), (1, 2)]
 POS = {o: i for i, o in enumerate(OFFSETS)}
+ROUND_Y = (1, 2)
 CHUNKS = [(0, 2), (2, 8), (8, 12), (12, 16)]
+HALVES = [(0, 8), (8, 16)]
 PARTS = [(0, 8), (8, 12), (12, 16)]
 QB = 512
 KB = 512
 
+SCHEDULE = [
+    "M0 gs0 gy0 gx0",
+    "M1 gs1 M2 gs2",
+    "P00 ks0 k1a0 k1b0",
+    "fya0 fyb0 gx1 k1c0",
+    "fx0 k2a0 k2b0 f20",
+    "P01 kd0 ks1 gy1",
+    "f3a0 f3b0 fx1 k1a1",
+    "k1b1 P02 ks2 fya1",
+    "fyb1 f40 k1c1 w0",
+    "P10 k1a2 gy2 k1b2",
+    "P03 ks3 A0o04 0@w1c",
+    "1@f3a1 1@f3b1 1@k1c2 2@f21",
+    "2@gx2 w1b k1c3 k2b1",
+    "k2a1 k1a3 k1b3 f41",
+    "w1a fx2 k2a2 k2b2",
+    "fya2 w2 P11 A1o04",
+    "0@w3 0@fyb2 P20 f3b2",
+    "kd1 kd2 A2002 0@f22",
+    "0@f3a2 0@k2a3 0@k2b3 A1004",
+    "f42 kd3 A1104 P21",
+    "A2024 2@w4a 2@w4b A2o04",
+    "A2104 2@w5 wd",
+]
+
 
 def kernel(
-    key_lat, inf_lat, key_steps, inf_steps, bounds, shift, scale, gate, wq, wk, wv, wo, qgain, kgain,
+    key_lat, inf_lat_hbm, key_steps, inf_steps, bounds, shift, scale, gate_hbm, wq, wk, wv, wo, qgain, kgain,
     key_out, inf_out,
-    G, KV0, KV1, KV2, KO, Q, ACC, ATT, AR, W,
-    g_send, g_recv, k_send, k_recv, a_send, a_recv,
+    G, WG, KV0, KV1, KV2, KO, Q, ACC, ATT, AR, W, inf_lat, gate,
+    g_send, g_recv, w_send, w_recv, k_send, k_recv, a_send, a_recv, loaded,
 ):
     seg, seq = lax.axis_index("seg"), lax.axis_index("seq")
     xh, z = seg // 4, seg % 4
@@ -46,6 +73,17 @@
     barrier = pltpu.get_barrier_semaphore()
     for peer in peers:
         pl.semaphore_signal(barrier, inc=1, device_id=peer, device_id_type=MESH)
+
+    loads = [
+        pltpu.make_async_copy(wq, W.at[:, pl.ds(0, HEAD)], loaded.at[0]),
+        pltpu.make_async_copy(wk, W.at[:, pl.ds(HEAD, HEAD)], loaded.at[1]),
+        pltpu.make_async_copy(wv, W.at[:, pl.ds(2 * HEAD, HEAD)], loaded.at[2]),
+        pltpu.make_async_copy(inf_lat_hbm, inf_lat, loaded.at[3]),
+        pltpu.make_async_copy(wo, WG.at[0, 0], loaded.at[4]),
+        pltpu.make_async_copy(gate_hbm, gate, loaded.at[5]),
+    ]
+    for load in loads:
+        load.start()
 
     def g_copy(f, src, to, dst, sem, rows=None):
         a, b = G.at[f, src], G.at[f, dst]
@@ -82,6 +120,8 @@
         took(f, S[0, 3])
         send(f, S[0, 3], (0, 1, 0), S[0, 2], rows=LOW)
         sib(f, (0, 3))
+
+    def g_fwd_y2(f):
         took(f, S[0, 1])
         send(f, S[0, 1], (0, 3, 0), S[0, 2], sem=16, rows=HIGH)
         sib(f, (0, 1))
@@ -95,22 +135,110 @@
     def g_fwd_2(f):
         took(f, S[0, 2], rows=LOW)
         took(f, S[0, 2], sem=16, rows=HIGH)
-        send(f, S[0, 2], (1, 0, 0), S[1, 2])
+        if f not in ROUND_Y:
+            send(f, S[0, 2], (1, 0, 0), S[1, 2])
         sib(f, (0, 2))
 
     def g_fwd_3(f):
         took(f, S[1, 3])
+        if f in ROUND_Y:
+            send(f, S[1, 3], (0, 1, 0), S[1, 2], rows=LOW)
         sib(f, (1, 3))
+
+    def g_fwd_32(f):
         took(f, S[1, 1])
+        if f in ROUND_Y:
+            send(f, S[1, 1], (0, 3, 0), S[1, 2], sem=17, rows=HIGH)
         sib(f, (1, 1))
 
     def g_fwd_4(f):
-        took(f, S[1, 2])
+        if f in ROUND_Y:
+            took(f, S[1, 2], rows=LOW)
+            took(f, S[1, 2], sem=17, rows=HIGH)
+        else:
+            took(f, S[1, 2])
         sib(f, (1, 2))
 
     def g_sib(f, lo, hi):
         for r in range(lo, hi, 2):
             took(f, r + 1)
+
+    def quarter(dz, part=0, parts=1):
+        size = TOK // 4 // parts
+        return pl.ds(pl.multiple_of(((z + dz) % 4) * (TOK // 4) + part * size, 16), size)
+
+    def w_copy(src, dst, sem, to):
+        return pltpu.make_async_remote_copy(
+            src_ref=src, dst_ref=dst, send_sem=w_send, recv_sem=w_recv.at[sem], device_id=to, device_id_type=MESH
+        )
+
+    def w_seq(a, b, sem, to=(0, 1, 0), half=None):
+        rows = quarter(0) if half is None else quarter(0, half, 2)
+        return w_copy(WG.at[0, POS[a], rows], WG.at[0, POS[b], rows], sem, at_seq(*to))
+
+    def w_seg(dz, sem, to=1, lo=1, hi=8):
+        ref = WG.at[0, pl.ds(lo, hi - lo), quarter(dz)]
+        return w_copy(ref, ref, sem, at_seg(0, to))
+
+    def w_sib(dz):
+        rows = quarter(dz)
+        return w_copy(WG.at[0, pl.ds(1, 7), rows], WG.at[1, pl.ds(1, 7), rows], 13 + dz, at_seq(0, 0, 1))
+
+    def w_sib_own():
+        return w_copy(WG.at[0, 0], WG.at[1, 0], 12, at_seq(0, 0, 1))
+
+    def w_0():
+        need(4)
+        w_sib_own().start()
+        w_seq((0, 0), (0, 3), 0, (0, 1, 0)).start()
+        w_seq((0, 0), (0, 1), 1, (0, 3, 0)).start()
+        w_seq((0, 0), (1, 0), 2, (1, 0, 0)).start()
+
+    def w_1():
+        w_seq((0, 3), (0, 3), 0).wait_recv()
+        w_seq((0, 3), (0, 2), 3, (0, 1, 0), 0).start()
+
+    def w_1b():
+        w_seq((0, 1), (0, 1), 1).wait_recv()
+        w_seq((0, 1), (0, 2), 4, (0, 3, 0), 1).start()
+
+    def w_1c():
+        w_seq((1, 0), (1, 0), 2).wait_recv()
+        w_seq((1, 0), (1, 3), 5, (0, 1, 0)).start()
+        w_seq((1, 0), (1, 1), 6, (0, 3, 0)).start()
+
+    def w_2():
+        w_seq((0, 2), (0, 2), 3, half=0).wait_recv()
+        w_seq((0, 2), (0, 2), 4, half=1).wait_recv()
+        w_seq((0, 2), (1, 2), 7, (1, 0, 0)).start()
+
+    def w_3():
+        w_seq((1, 3), (1, 3), 5).wait_recv()
+        w_seq((1, 1), (1, 1), 6).wait_recv()
+        w_seq((1, 2), (1, 2), 7).wait_recv()
+        w_seg(0, 8, 1).start()
+        w_seg(0, 9, 3).start()
+        w_sib(0).start()
+
+    def w_4():
+        w_seg(3, 8).wait_recv()
+        w_seg(3, 10, 1, 1, 5).start()
+        w_sib(3).start()
+
+    def w_4b():
+        w_seg(1, 9).wait_recv()
+        w_seg(1, 11, 3, 5, 8).start()
+        w_sib(1).start()
+
+    def w_5():
+        w_seg(2, 10, 1, 1, 5).wait_recv()
+        w_seg(2, 11, 3, 5, 8).wait_recv()
+        w_sib(2).start()
+
+    def w_done():
+        w_sib_own().wait_recv()
+        for dz in range(4):
+            w_sib(dz).wait_recv()
 
     KV = [KV0, KV1, KV2]
 
@@ -139,18 +267,24 @@
         k_copy(m, 0, (0, 1), POS[0, 3], POS[0, 3]).start()
         k_copy(m, 0, (0, 3), POS[0, 1], POS[0, 1]).start()
 
-    def k_fwd_1(m):
+    def k_fwd_1a(m):
         k_took(m, POS[0, 3])
         k_copy(m, POS[0, 3], (0, 1), POS[0, 2], POS[0, 2], 0).start()
+
+    def k_fwd_1b(m):
         k_took(m, POS[0, 1])
         k_copy(m, POS[0, 1], (0, 3), POS[0, 2], 8, 1).start()
+
+    def k_fwd_1c(m):
         k_took(m, POS[1, 0])
         k_copy(m, POS[1, 0], (0, 1), POS[1, 3], POS[1, 3]).start()
         k_copy(m, POS[1, 0], (0, 3), POS[1, 1], POS[1, 1]).start()
 
-    def k_fwd_2(m):
+    def k_fwd_2a(m):
         k_took(m, POS[1, 3])
         k_copy(m, POS[1, 3], (0, 1), POS[1, 2], POS[1, 2], 0).start()
+
+    def k_fwd_2b(m):
         k_took(m, POS[1, 1])
         k_copy(m, POS[1, 1], (0, 3), POS[1, 2], 9, 1).start()
 
@@ -177,11 +311,14 @@
     kg = kgain[...].reshape(1, HEAD)
 
     def project(f, lo, hi):
-        @pl.loop(lo // 2, hi // 2)
+        step = 4 if (hi - lo) % 4 == 0 else hi - lo
+        size = step * TOK
+
+        @pl.loop(0, (hi - lo) // step)
         def _(i):
-            x = G[f, pl.ds(2 * i, 2)].reshape(2 * TOK, D)
+            x = G[f, pl.ds(lo + step * i, step)].reshape(size, D)
             r = jnp.dot(x, W[...], preferred_element_type=jnp.float32)
-            rows = pl.ds(pl.multiple_of(i * 2 * TOK, 2 * TOK), 2 * TOK)
+            rows = pl.ds(pl.multiple_of(lo * TOK + i * size, 2 * TOK), size)
 
             def norm(t, gain):
                 return (t * lax.rsqrt(jnp.mean(t * t, axis=-1, keepdims=True) + EPSILON) * gain).astype(jnp.bfloat16)
@@ -190,7 +327,7 @@
             kv = jnp.concatenate([norm(r[:, HEAD : 2 * HEAD], kg), r[:, 2 * HEAD :].astype(jnp.bfloat16)], axis=1)
             if f == 0:
                 part, base = part_of(lo)
-                part[0, pl.ds(pl.multiple_of((i - base // 2) * 2 * TOK, 2 * TOK), 2 * TOK), :] = kv
+                part[0, pl.ds(pl.multiple_of((lo - base) * TOK + i * size, 2 * TOK), size), :] = kv
             else:
                 KO[f - 1, rows, :] = kv
 
@@ -198,13 +335,13 @@
 
     def a_copy(f, r):
         o = OFFSETS[r // 2]
-        back = 2 * POS[o[0], (4 - o[1]) % 4] + r % 2
+        back = (r % 2) * (SLOTS // 2) + POS[o[0], (4 - o[1]) % 4]
         return pltpu.make_async_remote_copy(
             src_ref=ATT.at[f, r], dst_ref=AR.at[f, :, pl.ds(back * HEAD, HEAD)], send_sem=a_send.at[f],
             recv_sem=a_recv.at[f], device_id=at_seq(*o, r % 2), device_id_type=MESH,
         )
 
-    def attend(f, lo, hi, sources, first, last, hooks=None):
+    def attend(f, lo, hi, sources, first, last, between):
         @pl.loop(lo, hi)
         def _(i):
             rows = pl.ds(pl.multiple_of(i * QB, QB), QB)
@@ -233,12 +370,8 @@
                             else:
                                 a_copy(f, r).start()
 
-            for n, hook in (hooks or {}).items():
-
-                @pl.when(i == n)
-                def _(hook=hook):
-                    for h in hook:
-                        h[0](*h[1:])
+            for n, then in between.items():
+                pl.when(i == n)(then)
 
     def own(f):
         if f == 0:
@@ -274,7 +407,7 @@
         @pl.loop(0, D // 256)
         def _(n):
             cols = pl.ds(pl.multiple_of(n * 256, 256), 256)
-            w = G[3, :, :, cols].reshape(SLOTS * TOK, 256)
+            w = WG[:, :, :, cols].reshape(SLOTS * TOK, 256)
             t = jnp.dot(x, w, preferred_element_type=jnp.float32)
             for f in range(3):
                 s = key_steps[0] if f == 0 else inf_steps[0, f - 1]
@@ -286,77 +419,59 @@
                 else:
                     inf_out[0, f - 1, :, cols] = o
 
-    modulate(0)
-    pl.semaphore_wait(barrier, len(peers))
-    g_send_sib(0)
-    g_send_y(0)
-    g_send_x(0)
-    W[:, :HEAD] = wq[...]
-    W[:, HEAD : 2 * HEAD] = wk[...]
-    W[:, 2 * HEAD :] = wv[...]
-    modulate(1)
-    g_send_sib(1)
-    g_sib(0, 0, 2)
-    project(0, 0, 2)
-    k_send_0(0)
-    modulate(2)
-    g_send_sib(2)
-    G[3, 0] = wo[...]
-    g_send_sib(3)
-
-    g_fwd_y(0)
-    g_fwd_x(0)
-    g_send_x(1)
-    k_fwd_1(0)
-    g_sib(0, 2, 8)
-    project(0, 2, 8)
-    k_send_0(1)
-    g_fwd_2(0)
-    k_fwd_2(0)
-    g_send_y(1)
-    g_fwd_3(0)
-    k_fwd_1(1)
-    g_sib(0, 8, 12)
-    project(0, 8, 12)
-    k_send_0(2)
-    g_fwd_4(0)
-    g_sib(0, 12, 16)
-    project(0, 12, 16)
-    k_send_0(3)
-    g_send_x(2)
-    attend(0, 0, 4, own(0), True, True, {1: [(g_fwd_y, 1), (g_fwd_x, 1)], 2: [(k_fwd_2, 1)]})
-    g_sib(1, 0, 8)
-    project(1, 0, 8)
-    g_fwd_2(1)
-    g_send_y(2)
-    k_fwd_1(2)
-    k_done(0)
-    k_done(1)
-    attend(1, 0, 2, cond(0), True, False, {0: [(g_fwd_3, 1)]})
-    g_fwd_4(1)
-    g_send_x(3)
-    k_fwd_2(2)
-    g_sib(1, 8, 16)
-    project(1, 8, 16)
-    attend(1, 0, 2, own(1), False, False, {0: [(g_fwd_y, 2), (g_fwd_x, 2)]})
-    k_fwd_1(3)
-    attend(1, 2, 4, own(1), True, False, {2: [(g_fwd_2, 2)]})
-    g_send_y(3)
-    g_sib(2, 0, 8)
-    project(2, 0, 8)
-    k_done(2)
-    attend(1, 2, 4, cond(0), False, False, {2: [(k_fwd_2, 3)]})
-    attend(2, 0, 2, cond(0), True, False, {0: [(g_fwd_3, 2)]})
-    g_fwd_4(2)
-    g_sib(2, 8, 16)
-    project(2, 8, 16)
-    attend(2, 0, 2, own(2), False, False, {0: [(g_fwd_y, 3), (g_fwd_x, 3)]})
-    attend(2, 2, 4, own(2), True, False, {2: [(g_fwd_2, 3)]})
-    attend(2, 2, 4, cond(0), False, False)
-    k_done(3)
-    attend(1, 0, 4, cond(1, 2), False, True, {1: [(g_fwd_3, 3)], 3: [(g_fwd_4, 3)]})
-    attend(2, 0, 4, cond(1, 2), False, True)
-    g_sib(3, 0, 16)
+    waited, begun = set(), set()
+
+    def need(*which):
+        for n in which:
+            if n not in waited:
+                waited.add(n)
+                loads[n].wait()
+
+    def do_modulate(f):
+        if f:
+            need(3)
+        modulate(f)
+        if f == 0:
+            pl.semaphore_wait(barrier, len(peers))
+
+    def do_project(f, n):
+        need(0, 1, 2)
+        lo, hi = (CHUNKS if f == 0 else HALVES)[n]
+        g_sib(f, lo, hi)
+        project(f, lo, hi)
+
+    def do_attend(f, what, lo, hi, between):
+        first = (f, lo) not in begun
+        begun.update((f, i) for i in range(lo, hi))
+        parts = {"o": own(f), "0": cond(0), "1": cond(1, 2)}[what]
+        attend(f, lo, hi, parts, first, f == 0 or what == "1", between)
+
+    simple = dict(
+        gs=g_send_sib, gy=g_send_y, gx=g_send_x, fya=g_fwd_y, fyb=g_fwd_y2, fx=g_fwd_x, f2=g_fwd_2, f3a=g_fwd_3,
+        f3b=g_fwd_32, f4=g_fwd_4, ks=k_send_0, k1a=k_fwd_1a, k1b=k_fwd_1b, k1c=k_fwd_1c, k2a=k_fwd_2a, k2b=k_fwd_2b,
+        kd=k_done, M=do_modulate,
+    )
+    whole_w = dict(w0=w_0, w1a=w_1, w1b=w_1b, w1c=w_1c, w2=w_2, w3=w_3, w4a=w_4, w4b=w_4b, w5=w_5, wd=w_done)
+
+    def run(op, between=()):
+        if op in whole_w:
+            whole_w[op]()
+        elif op[0] == "P":
+            do_project(int(op[1]), int(op[2]))
+        elif op[0] == "A":
+            steps = {n: [b[2:] for b in between if int(b[0]) == n] for n in {int(b[0]) for b in between}}
+            thens = {n: lambda ops=ops: [run(o) for o in ops] and None for n, ops in steps.items()}
+            do_attend(int(op[1]), op[2], int(op[3]), int(op[4]), thens)
+        else:
+            simple[op[:-1]](int(op[-1]))
+
+    todo = [op for line in SCHEDULE for op in line.split()]
+    while todo:
+        op, inside = todo.pop(0), []
+        while todo and todo[0][1] == "@":
+            inside.append(todo.pop(0))
+        run(op, inside)
+    need(5)
     for f in range(3):
         whole = AR.at[f, :, pl.ds(HEAD, (SLOTS - 1) * HEAD)]
         pltpu.make_async_remote_copy(
@@ -365,12 +480,14 @@
         ).wait_recv()
     finish()
 
-    for f in range(4):
+    for f in range(3):
         sent = G.at[f, pl.ds(0, 15)]
         pltpu.make_async_remote_copy(
             src_ref=sent, dst_ref=sent, send_sem=g_send.at[f], recv_sem=g_recv.at[f, 0],
             device_id=at_seq(0, 1, 0), device_id_type=MESH,
         ).wait_send()
+    sent = G.at[0, pl.ds(0, 15)]
+    w_copy(sent, sent, 0, at_seq(0, 1, 0)).wait_send()
     for m, (lo, hi) in enumerate(CHUNKS):
         part, base = part_of(lo)
         sent = part.at[pl.ds(0, 7), pl.ds((lo - base) * TOK, (hi - lo) * TOK)]
@@ -391,6 +508,7 @@
     query_weight, key_weight, value_weight, out_weight, query_gain, key_gain,
 ):
     vmem, smem = pl.BlockSpec(memory_space=pltpu.VMEM), pl.BlockSpec(memory_space=pltpu.SMEM)
+    hbm = pl.BlockSpec(memory_space=pl.ANY)
     bf16, f32 = jnp.bfloat16, jnp.float32
     n_tok = SLOTS * TOK
     return pl.pallas_call(
@@ -400,10 +518,11 @@
             jax.ShapeDtypeStruct(keyframe_latents.shape, bf16),
             jax.ShapeDtypeStruct(infill_latents.shape, bf16),
         ),
-        in_specs=[vmem, vmem, smem, smem, smem] + [vmem] * 9,
+        in_specs=[vmem, hbm, smem, smem, smem, vmem, vmem, hbm, hbm, hbm, hbm, hbm, vmem, vmem],
         out_specs=(vmem, vmem),
         scratch_shapes=[
-            pltpu.VMEM((4, SLOTS, TOK, D), bf16),
+            pltpu.VMEM((3, SLOTS, TOK, D), bf16),
+            pltpu.VMEM((2, SLOTS // 2, TOK, D), bf16),
             *[pltpu.VMEM((8, (hi - lo) * TOK, 2 * HEAD), bf16) for lo, hi in PARTS],
             pltpu.VMEM((2, n_tok, 2 * HEAD), bf16),
             pltpu.VMEM((3, n_tok, HEAD), bf16),
@@ -411,12 +530,17 @@
             pltpu.VMEM((3, SLOTS, TOK, HEAD), bf16),
             pltpu.VMEM((3, TOK, SLOTS * HEAD), bf16),
             pltpu.VMEM((D, 3 * HEAD), bf16),
-            pltpu.SemaphoreType.DMA((4,)),
-            pltpu.SemaphoreType.DMA((4, 17)),
+            pltpu.VMEM(infill_latents.shape, bf16),
+            pltpu.VMEM(gate_table.shape, f32),
+            pltpu.SemaphoreType.DMA((3,)),
+            pltpu.SemaphoreType.DMA((3, 18)),
+            pltpu.SemaphoreType.DMA,
+            pltpu.SemaphoreType.DMA((17,)),
             pltpu.SemaphoreType.DMA((4,)),
             pltpu.SemaphoreType.DMA((4, 10)),
             pltpu.SemaphoreType.DMA((3,)),
             pltpu.SemaphoreType.DMA((3,)),
+            pltpu.SemaphoreType.DMA((6,)),
         ],
         compiler_params=pltpu.CompilerParams(
             collective_id=0, has_side_effects=True, vmem_limit_bytes=62 * 2**20

time: 150 us -> 144 us (0.960)
  Pallas kernels: 146 us -> 140 us
    pallas_call x1, Pallas kernels: 146 us -> 140 us  [local(): pl.pallas_call(kernel, name='diffusion_block', out_shape=(jax.ShapeDtypeS...]
where the time goes in v2:
time: 144 us
  Pallas kernels  140 us (97%)
  local copies, waits for them, and re-layouts  2.72 us (2%)
    pallas_call x1, Pallas kernels, local(): pl.pallas_call(kernel, name='diffusion_block', out_shape=(jax.ShapeDtypeS...  140 us

profile of v2, /device:TPU:1, one launch (start us, length us, event | category | flops | bytes accessed | tf_op | source)
XLA Modules:
  0.0 143.7 jit_solution(13235950219673211736)
XLA Ops:
  1.3 139.7 %diffusion_block.1 = (bf16[1,128,1536]{2,1,0:T(8,128)(2,1)}, bf16[1,2,128,1536]{3,2,1,0:T(8,128)(2,1)}) custom-call(bf16[1,128,1536]{2,1,0:T(8,128)(2,1)} %key_lat.1, bf16[1,2,128,1536]{3,2,1,0:T(8,128)(2,1)} %inf_lat_hbm.1, s32[1]{0:T(128)S(6)} %copy.18.key_steps, s32[1,2]{1,0:T(1,128)} %inf_steps.1, s32[1,2]{1,0:T(1,128)} %bounds.1, f32[64,1536]{1,0:T(8,128)} %shift.1, ...), custom_call_target="tpu_custom_call" | custom-call | tf_op jit(solution)/shard_map/diffusion_block/pallas_call | solution.py:514
  141.0 0.0 copy-start
  141.0 1.8 %copy.19 = bf16[1,128,1536]{2,1,0:T(8,128)(2,1)} copy(bf16[1,128,1536]{2,1,0:T(8,128)(2,1)} %get-tuple-element.4) | data formatting | bytes 786432
  142.8 0.0 copy-done
  142.8 0.9 copy.20
Async XLA Ops:
  141.0 1.9 %copy-start = (bf16[1,2,128,1536]{3,2,1,0:T(8,128)(2,1)S(1)}, bf16[1,2,128,1536]{3,2,1,0:T(8,128)(2,1)}, u32[]{:S(2)}) copy-start(bf16[1,2,128,1536]{3,2,1,0:T(8,128)(2,1)} %get-tuple-element.5) | copy-start | bytes 2359300

commit v3 on v2

--- a/solution.py
+++ b/solution.py
@@ -29,23 +29,26 @@
     "P00 ks0 k1a0 k1b0",
     "fya0 fyb0 gx1 k1c0",
     "fx0 k2a0 k2b0 f20",
-    "P01 kd0 ks1 gy1",
+    "P01 kd0 gy1 ks1",
     "f3a0 f3b0 fx1 k1a1",
     "k1b1 P02 ks2 fya1",
-    "fyb1 f40 k1c1 w0",
+    "fyb1 f40 k1c1 gx2",
     "P10 k1a2 gy2 k1b2",
-    "P03 ks3 A0o04 0@w1c",
-    "1@f3a1 1@f3b1 1@k1c2 2@f21",
-    "2@gx2 w1b k1c3 k2b1",
-    "k2a1 k1a3 k1b3 f41",
-    "w1a fx2 k2a2 k2b2",
-    "fya2 w2 P11 A1o04",
-    "0@w3 0@fyb2 P20 f3b2",
-    "kd1 kd2 A2002 0@f22",
-    "0@f3a2 0@k2a3 0@k2b3 A1004",
-    "f42 kd3 A1104 P21",
-    "A2024 2@w4a 2@w4b A2o04",
-    "A2104 2@w5 wd",
+    "w0 A1a02 f21 f3a1",
+    "f3b1 P03 k1c2 ks3",
+    "A0o04 2@w1a k2b1 k2a1",
+    "f41 k2a2 fyb2 k2b2",
+    "k1a3 k1b3 w1b w1c",
+    "fx2 P11 fya2 A1b02",
+    "A1b24 kd1 w2 k1c3",
+    "A1a24 P20 kd2 w3",
+    "A1104 A2102 0@f22 A2002",
+    "f3a2 f3b2 k2a3 k2b3",
+    "A2a02 A1004 2@f42 kd3",
+    "A1224 A1202 P21 A2024",
+    "2@w4a 2@w4b A2b02 A2202",
+    "A2224 A2124 A2a24 A2b24",
+    "2@w5 wd",
 ]
 
 
@@ -299,9 +302,9 @@
         gain = 1.0 + scale[pl.ds(step, 1), :]
         move = shift[pl.ds(step, 1), :]
 
-        @pl.loop(0, TOK, step=32)
+        @pl.loop(0, TOK, step=64)
         def _(r):
-            rows = pl.ds(r, 32)
+            rows = pl.ds(r, 64)
             x = (key_lat[0, rows, :] if f == 0 else inf_lat[0, f - 1, rows, :]).astype(jnp.float32)
             x = x - jnp.mean(x, axis=-1, keepdims=True)
             x = x * lax.rsqrt(jnp.mean(x * x, axis=-1, keepdims=True) + EPSILON)
@@ -373,14 +376,17 @@
             for n, then in between.items():
                 pl.when(i == n)(then)
 
-    def own(f):
+    def own(f, part=0):
         if f == 0:
             return [
                 lambda n=n, j=j: KV[n][0, j * KB : (j + 1) * KB, :]
                 for n, (lo, hi) in enumerate(PARTS)
                 for j in range((hi - lo) * TOK // KB)
             ]
-        return [lambda j=j: KO[f - 1, j * KB : (j + 1) * KB, :] for j in range(SLOTS * TOK // KB)]
+        half = SLOTS * TOK // KB // 2
+        return [
+            lambda j=j: KO[f - 1, j * KB : (j + 1) * KB, :] for j in range(half * part, half * (part + 1))
+        ]
 
     def slot_of(k):
         kx, kz = k // 4, k % 4
@@ -404,10 +410,10 @@
     def finish():
         x = AR[...].reshape(3 * TOK, SLOTS * HEAD)
 
-        @pl.loop(0, D // 256)
+        @pl.loop(0, D // 768)
         def _(n):
-            cols = pl.ds(pl.multiple_of(n * 256, 256), 256)
-            w = WG[:, :, :, cols].reshape(SLOTS * TOK, 256)
+            cols = pl.ds(pl.multiple_of(n * 768, 256), 768)
+            w = WG[:, :, :, cols].reshape(SLOTS * TOK, 768)
             t = jnp.dot(x, w, preferred_element_type=jnp.float32)
             for f in range(3):
                 s = key_steps[0] if f == 0 else inf_steps[0, f - 1]
@@ -419,7 +425,7 @@
                 else:
                     inf_out[0, f - 1, :, cols] = o
 
-    waited, begun = set(), set()
+    waited, begun = set(), {}
 
     def need(*which):
         for n in which:
@@ -442,9 +448,10 @@
 
     def do_attend(f, what, lo, hi, between):
         first = (f, lo) not in begun
-        begun.update((f, i) for i in range(lo, hi))
-        parts = {"o": own(f), "0": cond(0), "1": cond(1, 2)}[what]
-        attend(f, lo, hi, parts, first, f == 0 or what == "1", between)
+        parts = {"o": (own, f), "a": (own, f, 0), "b": (own, f, 1), "0": (cond, 0), "1": (cond, 1), "2": (cond, 2)}[what]
+        for i in range(lo, hi):
+            begun[f, i] = begun.get((f, i), 0) + 1
+        attend(f, lo, hi, parts[0](*parts[1:]), first, f == 0 or begun[f, lo] == 5, between)
 
     simple = dict(
         gs=g_send_sib, gy=g_send_y, gx=g_send_x, fya=g_fwd_y, fyb=g_fwd_y2, fx=g_fwd_x, f2=g_fwd_2, f3a=g_fwd_3,

time: 144 us -> 141 us (0.979)
  Pallas kernels: 140 us -> 137 us
    pallas_call x1, Pallas kernels: 140 us -> 137 us  [local(): pl.pallas_call(kernel, name='diffusion_block', out_shape=(jax.ShapeDtypeS...]
where the time goes in v3:
time: 141 us
  Pallas kernels  137 us (97%)
  local copies, waits for them, and re-layouts  2.72 us (2%)
    pallas_call x1, Pallas kernels, local(): pl.pallas_call(kernel, name='diffusion_block', out_shape=(jax.ShapeDtypeS...  137 us

profile of v3, /device:TPU:1, one launch (start us, length us, event | category | flops | bytes accessed | tf_op | source)
XLA Modules:
  0.0 141.1 jit_solution(14282872635331134698)
XLA Ops:
  1.3 137.1 %diffusion_block.1 = (bf16[1,128,1536]{2,1,0:T(8,128)(2,1)}, bf16[1,2,128,1536]{3,2,1,0:T(8,128)(2,1)}) custom-call(bf16[1,128,1536]{2,1,0:T(8,128)(2,1)} %key_lat.1, bf16[1,2,128,1536]{3,2,1,0:T(8,128)(2,1)} %inf_lat_hbm.1, s32[1]{0:T(128)S(6)} %copy.18.key_steps, s32[1,2]{1,0:T(1,128)} %inf_steps.1, s32[1,2]{1,0:T(1,128)} %bounds.1, f32[64,1536]{1,0:T(8,128)} %shift.1, ...), custom_call_target="tpu_custom_call" | custom-call | tf_op jit(solution)/shard_map/diffusion_block/pallas_call | solution.py:521
  138.4 0.0 copy-start
  138.4 1.8 %copy.19 = bf16[1,128,1536]{2,1,0:T(8,128)(2,1)} copy(bf16[1,128,1536]{2,1,0:T(8,128)(2,1)} %get-tuple-element.4) | data formatting | bytes 786432
  140.2 0.0 copy-done
  140.2 0.9 copy.20
Async XLA Ops:
  138.4 1.9 %copy-start = (bf16[1,2,128,1536]{3,2,1,0:T(8,128)(2,1)S(1)}, bf16[1,2,128,1536]{3,2,1,0:T(8,128)(2,1)}, u32[]{:S(2)}) copy-start(bf16[1,2,128,1536]{3,2,1,0:T(8,128)(2,1)} %get-tuple-element.5) | copy-start | bytes 2359300

commit v4 on v3

--- a/solution.py
+++ b/solution.py
@@ -21,7 +21,7 @@
 HALVES = [(0, 8), (8, 16)]
 PARTS = [(0, 8), (8, 12), (12, 16)]
 QB = 512
-KB = 512
+KB = 256
 
 SCHEDULE = [
     "M0 gs0 gy0 gx0",

time: 141 us -> 140 us (level)
  no operation moved by 1% of the time
where the time goes in v4:
time: 140 us
  Pallas kernels  136 us (97%)
  local copies, waits for them, and re-layouts  2.72 us (2%)
    pallas_call x1, Pallas kernels, local(): pl.pallas_call(kernel, name='diffusion_block', out_shape=(jax.ShapeDtypeS...  136 us

profile of v4, /device:TPU:1, one launch (start us, length us, event | category | flops | bytes accessed | tf_op | source)
XLA Modules:
  0.0 140.1 jit_solution(18233164942391864821)
XLA Ops:
  1.3 136.1 %diffusion_block.1 = (bf16[1,128,1536]{2,1,0:T(8,128)(2,1)}, bf16[1,2,128,1536]{3,2,1,0:T(8,128)(2,1)}) custom-call(bf16[1,128,1536]{2,1,0:T(8,128)(2,1)} %key_lat.1, bf16[1,2,128,1536]{3,2,1,0:T(8,128)(2,1)} %inf_lat_hbm.1, s32[1]{0:T(128)S(6)} %copy.18.key_steps, s32[1,2]{1,0:T(1,128)} %inf_steps.1, s32[1,2]{1,0:T(1,128)} %bounds.1, f32[64,1536]{1,0:T(8,128)} %shift.1, ...), custom_call_target="tpu_custom_call" | custom-call | tf_op jit(solution)/shard_map/diffusion_block/pallas_call | solution.py:521
  137.4 0.0 copy-start
  137.4 1.8 %copy.19 = bf16[1,128,1536]{2,1,0:T(8,128)(2,1)} copy(bf16[1,128,1536]{2,1,0:T(8,128)(2,1)} %get-tuple-element.4) | data formatting | bytes 786432
  139.3 0.0 copy-done
  139.3 0.9 copy.20
Async XLA Ops:
  137.4 1.9 %copy-start = (bf16[1,2,128,1536]{3,2,1,0:T(8,128)(2,1)S(1)}, bf16[1,2,128,1536]{3,2,1,0:T(8,128)(2,1)}, u32[]{:S(2)}) copy-start(bf16[1,2,128,1536]{3,2,1,0:T(8,128)(2,1)} %get-tuple-element.5) | copy-start | bytes 2359300
